TPU v7x, 256 devices: a whole 4x4x8 slice. The times are simulated.
256 devices in a mesh: outer: 8 (over z), inner: 32 (over x, y, core).
Axes of the slice: x: 4, y: 4, z: 8, core: 2. Of those that a mesh axis runs over, the one named last changes fastest.
Arguments:
- resid: bfloat16 [32768, 4096], P(('outer', 'inner')), may hold values from -30 to 30, as said below
- query_mr: bfloat16 [32768, 4096], P(('outer', 'inner')), may hold values from -6 to 6
- key_mr: bfloat16 [32768, 4096], P(('outer', 'inner')), may hold values from -6 to 6
- value_mr: bfloat16 [32768, 4096], P(('outer', 'inner')), may hold values from -6 to 6
- query_li: bfloat16 [32768, 4096], P(('outer', 'inner')), may hold values from -6 to 6
- key_li: bfloat16 [32768, 4096], P(('outer', 'inner')), may hold values from -6 to 6
- mr_filter: bfloat16 [128, 256], replicated, may hold values from -0.5 to 0.5
- pole_rate: float32 [16, 256], replicated, may hold values from 6.1035155e-07 to 0.05
- residue: float32 [16, 256], replicated, may hold values from -2.1 to 2.1
Outputs:
- mixed_mr: bfloat16 [32768, 4096], P(('outer', 'inner'))
- long_out: bfloat16 [32768, 4096], P(('outer', 'inner'))
Inputs may be any that keep to these rules, and one draw needn't show every extreme that they name: `resid`: activations of the residual stream.
All inputs are finite; a program needn't handle non-finite values.
Results may differ from a plain program's by a relative error of at most 0.006.
Values may be sent and summed in bfloat16 or wider, within the bound.
No kernel may reach another device: no remote copies, remote signals or barrier semaphores. Data moves between devices by JAX's collectives and lax.ppermute only.
A program may use at most 256 MiB of HBM per device.

v0:
```python
import functools

import jax
import jax.numpy as jnp
from jax import lax
from jax.experimental import pallas as pl
from jax.experimental.pallas import tpu as pltpu
from jax.sharding import PartitionSpec as P

EPSILON = 1e-06
AXES = ("outer", "inner")
LANES = 128
HALF = LANES // 2
SUB = 32
PARTS = 4
LARGE = 58 * 1024 * 1024
SMALL = 4 * 1024 * 1024
F32 = jnp.float32
BF16 = jnp.bfloat16
VMEM = pl.BlockSpec(memory_space=pltpu.VMEM)
HBM = pl.BlockSpec(memory_space=pltpu.HBM)
SMEM = pl.BlockSpec(memory_space=pltpu.SMEM)


def from_behind(block, axis, distance):
    devices = range(lax.axis_size(axis))
    route = [(i - distance, i) for i in devices if i - distance in devices]
    return lax.ppermute(block, axis, route)


def span(index, size):
    return pl.ds(pl.multiple_of(index * size, size), size)


def own_lanes(stack, rows, groups, per_group):
    group = lax.broadcasted_iota(jnp.int32, (rows, LANES), 1) % (groups * per_group) // per_group
    out = stack[:rows]
    for g in range(1, groups):
        out = jnp.where(group == g, stack[g * rows : (g + 1) * rows], out)
    return out


def half_turn(block):
    return jnp.concatenate([block[:, HALF:], block[:, :HALF]], axis=1)


def causal(table, old, new, per_group):
    rows = new.shape[0]

    def window(before, now, b):
        return jnp.concatenate([before[b * SUB :], now[: (b + 1) * SUB]], axis=0)

    old_turned, new_turned = half_turn(old), half_turn(new)
    depth = rows + SUB
    low = lax.broadcasted_iota(jnp.int32, (depth, LANES), 1) < HALF
    first, second = [], []
    for b in range(0, rows // SUB, 2):
        straight, turned = window(old, new, b), window(old_turned, new_turned, b + 1)
        first.append(jnp.where(low, straight, turned))
        second.append(jnp.where(low, turned, straight))
    middle = table.shape[0] // 2
    stack_a = jnp.dot(table[:middle], jnp.concatenate(first, axis=1), preferred_element_type=F32)
    stack_b = jnp.dot(table[middle:], jnp.concatenate(second, axis=1), preferred_element_type=F32)
    low = lax.broadcasted_iota(jnp.int32, (SUB, LANES), 1) < HALF
    out = []
    for j in range(rows // SUB // 2):
        cols = slice(j * LANES, (j + 1) * LANES)
        a = own_lanes(stack_a[:, cols], SUB, HALF // per_group, per_group)
        b = own_lanes(stack_b[:, cols], SUB, HALF // per_group, per_group)
        out.append(jnp.where(low, a, b))
        out.append(pltpu.roll(jnp.where(low, b, a), HALF, 1))
    return out


def table_kernel(per_group, medium_taps_ref, long_taps_ref, medium_hbm, long_hbm, medium_ref, long_ref, sems):
    groups = LANES // per_group
    slabs = medium_ref.shape[0]
    row = lax.broadcasted_iota(jnp.int32, (SUB, LANES), 0)
    lane = lax.broadcasted_iota(jnp.int32, (SUB, LANES), 1)
    copies = []
    for i, (taps_ref, table_ref, out_hbm) in enumerate(
        ((medium_taps_ref, medium_ref, medium_hbm), (long_taps_ref, long_ref, long_hbm))
    ):

        def fill(slab, _):
            taps = taps_ref[span(slab, groups), :]
            for g in range(groups):
                turned = pltpu.roll(jnp.broadcast_to(taps[g : g + 1, :], (SUB, LANES)), 0, 1, stride=1, stride_axis=0)
                rows = slice(g * SUB, (g + 1) * SUB)
                table_ref[slab, rows, :LANES] = jnp.where(lane > row, turned, 0.0).astype(BF16)
                table_ref[slab, rows, LANES:] = jnp.where(lane <= row, turned, 0.0)[:, :SUB].astype(BF16)
            return 0

        lax.fori_loop(0, slabs, fill, 0, unroll=4)
        copies.append(pltpu.make_async_copy(table_ref, out_hbm, sems.at[i]))
        copies[i].start()
    for copy in copies:
        copy.wait()


def medium_kernel(per_group, table_hbm, rim_hbm, product_hbm, query_hbm, resid_hbm, key_hbm, ending_hbm, long_hbm,
                  entering_hbm, mixed_hbm, gated_hbm, state_ref, table_ref, rim_ref, product_ref, query_ref, resid_ref,
                  key_ref, ending_ref, mixed_ref, gated_ref, square_ref, load_sems, late_sems, store_sems):
    rows, width = product_ref.shape
    slabs = width // LANES // PARTS

    def loads(part):
        cols = span(part, width // PARTS)
        several = pl.ds(part * slabs, slabs)
        pairs = [(table_hbm.at[several], table_ref.at[several])]
        pairs += [
            (source.at[:, cols], target.at[:, cols])
            for source, target in (
                (rim_hbm, rim_ref), (product_hbm, product_ref), (query_hbm, query_ref), (resid_hbm, resid_ref)
            )
        ]
        return [pltpu.make_async_copy(*pair, load_sems.at[part, i]) for i, pair in enumerate(pairs)]

    def store(source, target, part, which):
        cols = span(part, width // PARTS)
        return pltpu.make_async_copy(source.at[:, cols], target.at[:, cols], store_sems.at[which, part])

    late = [
        pltpu.make_async_copy(key_hbm, key_ref, late_sems.at[0]),
        pltpu.make_async_copy(ending_hbm, ending_ref, late_sems.at[1]),
    ]
    for part in range(PARTS):
        for copy in loads(part):
            copy.start()
    for copy in late:
        copy.start()
    square_ref[...] = jnp.zeros_like(square_ref)

    def mix(part, _):
        for copy in loads(part):
            copy.wait()

        def one(turn, _):
            slab = part * slabs + turn
            cols = span(slab, LANES)
            convolved = causal(table_ref[slab], rim_ref[:, cols], product_ref[:, cols], per_group)
            for b, sums in enumerate(convolved):
                block = slice(b * SUB, (b + 1) * SUB)
                mixed = (resid_ref[block, cols].astype(F32) + query_ref[block, cols].astype(F32) * sums).astype(BF16)
                mixed_ref[block, cols] = mixed
                stream = mixed.astype(F32)
                square_ref[block, :] += stream * stream
            return 0

        lax.fori_loop(0, slabs, one, 0, unroll=True)
        store(mixed_ref, mixed_hbm, part, 0).start()
        return 0

    lax.fori_loop(0, PARTS, mix, 0)
    mean = jnp.sum(square_ref[...], axis=1, keepdims=True) * (1.0 / width)
    square_ref[...] = jnp.broadcast_to(lax.rsqrt(mean + EPSILON), square_ref.shape)
    owners, poles, owned = state_ref.shape
    for copy in late:
        copy.wait()

    def gate(part, _):
        def one(turn, _):
            slab = part * slabs + turn
            cols = span(slab, LANES)
            gated = (key_ref[:, cols].astype(F32) * mixed_ref[:, cols].astype(F32) * square_ref[...]).astype(BF16)
            gated_ref[:, cols] = gated
            stack = jnp.dot(ending_ref[cols, :], gated, preferred_element_type=F32)
            state_ref[slab] = own_lanes(stack, poles, LANES // per_group, per_group).astype(BF16)
            return 0

        lax.fori_loop(0, slabs, one, 0, unroll=True)
        store(gated_ref, gated_hbm, part, 1).start()
        return 0

    lax.fori_loop(0, PARTS, gate, 0)
    for part in range(PARTS):
        store(mixed_ref, mixed_hbm, part, 0).wait()
        store(gated_ref, gated_hbm, part, 1).wait()


def local_kernel(per_group, table_hbm, gated_hbm, after_ref, local_hbm, token_ref, table_ref, gated_ref, local_ref,
                 load_sems, store_sems):
    rows, width = gated_ref.shape
    slabs = width // LANES // PARTS

    def loads(part):
        cols = span(part, width // PARTS)
        several = pl.ds(part * slabs, slabs)
        return [
            pltpu.make_async_copy(table_hbm.at[several], table_ref.at[several], load_sems.at[part, 0]),
            pltpu.make_async_copy(gated_hbm.at[:, cols], gated_ref.at[:, cols], load_sems.at[part, 1]),
        ]

    def store(part):
        cols = span(part, width // PARTS)
        return pltpu.make_async_copy(local_ref.at[:, cols], local_hbm.at[:, cols], store_sems.at[part])

    for part in range(PARTS):
        for copy in loads(part):
            copy.start()
    token_ref[...] = jnp.zeros_like(token_ref)

    def convolve(part, _):
        for copy in loads(part):
            copy.wait()

        def one(turn, _):
            slab = part * slabs + turn
            cols = span(slab, LANES)
            old = jnp.zeros((rows, LANES), BF16)
            for b, sums in enumerate(causal(table_ref[slab], old, gated_ref[:, cols], per_group)):
                local_ref[b * SUB : (b + 1) * SUB, cols] = sums
            return 0

        lax.fori_loop(0, slabs, one, 0, unroll=True)
        store(part).start()
        return 0

    lax.fori_loop(0, PARTS, convolve, 0)
    for part in range(PARTS):
        store(part).wait()


def total_kernel(states_ref, decay_ref, total_ref):
    decay = decay_ref[...]
    total = states_ref[0].astype(F32)
    for i in range(1, states_ref.shape[0]):
        total = decay * total + states_ref[i].astype(F32)
    total = total.astype(BF16)
    for i in range(total_ref.shape[0]):
        total_ref[i] = total


def enter_kernel(place_ref, states_ref, totals_ref, decay_ref, group_decay_ref, after_ref, entered_ref):
    place = place_ref[0]
    group_decay = group_decay_ref[...]

    def one(turn, state):
        return group_decay * state + totals_ref[turn].astype(F32)

    state = lax.fori_loop(0, place, one, jnp.zeros_like(group_decay))
    decay = decay_ref[...]
    for i in range(states_ref.shape[0]):
        entered_ref[i] = state.astype(BF16)
        if i + 1 < states_ref.shape[0]:
            state = decay * state + states_ref[i].astype(F32)


def final_kernel(per_group, entering_hbm, state_ref, local_hbm, query_hbm, out_hbm,
                 entering_ref, local_ref, query_ref, out_ref, load_sems, store_sems):
    owners, poles, owned = state_ref.shape
    width = owners * owned
    pair = 2
    steps = owners // pair // PARTS

    def loads(part):
        cols = span(part, width // PARTS)
        pairs = ((entering_hbm, entering_ref), (local_hbm, local_ref), (query_hbm, query_ref))
        return [
            pltpu.make_async_copy(source.at[:, cols], target.at[:, cols], load_sems.at[part, i])
            for i, (source, target) in enumerate(pairs)
        ]

    def store(part):
        cols = span(part, width // PARTS)
        return pltpu.make_async_copy(out_ref.at[:, cols], out_hbm.at[:, cols], store_sems.at[part])

    for part in range(PARTS):
        for copy in loads(part):
            copy.start()
    spread = pair * owned // per_group
    row_group = lax.broadcasted_iota(jnp.int32, (spread * poles, pair * owned), 0) // poles
    lane_group = lax.broadcasted_iota(jnp.int32, (spread * poles, pair * owned), 1) // per_group
    own = row_group == lane_group

    def finish(part, _):
        for copy in loads(part):
            copy.wait()

        def one(turn, _):
            slab = part * steps + turn
            cols = span(slab, pair * owned)
            state = jnp.concatenate([state_ref[slab * pair + i] for i in range(pair)], axis=1)
            diagonal = jnp.where(own, jnp.concatenate([state] * spread, axis=0), jnp.zeros((), BF16))
            carried = jnp.dot(entering_ref[:, cols], diagonal, preferred_element_type=F32)
            out_ref[:, cols] = (query_ref[:, cols].astype(F32) * (local_ref[:, cols] + carried)).astype(BF16)
            return 0

        lax.fori_loop(0, steps, one, 0, unroll=True)
        store(part).start()
        return 0

    lax.fori_loop(0, PARTS, finish, 0)
    for part in range(PARTS):
        store(part).wait()


def call(body, out, in_specs, out_specs, name, scratch=(), flops=0, moved=0, limit=LARGE):
    return pl.pallas_call(
        body,
        out_shape=out,
        in_specs=in_specs,
        out_specs=out_specs,
        scratch_shapes=scratch,
        name=name,
        cost_estimate=pl.CostEstimate(flops=flops, bytes_accessed=moved, transcendentals=0),
        compiler_params=pltpu.CompilerParams(vmem_limit_bytes=limit),
    )


def shards(resid, query_mr, key_mr, value_mr, query_li, key_li, mr_filter, pole_rate, residue):
    tap_count, group_count = mr_filter.shape
    poles = pole_rate.shape[0]
    rows, width = resid.shape
    per_group = width // group_count
    members = lax.axis_size("inner")
    teams = lax.axis_size("outer")
    owned = width // members
    shape = jax.ShapeDtypeStruct
    sems = pltpu.SemaphoreType.DMA

    product = (key_mr.astype(F32) * value_mr.astype(F32)).astype(BF16)
    rim = from_behind(product, AXES, 1)

    backward = (LANES - jnp.arange(LANES)) % LANES
    taps = mr_filter.astype(F32)
    taps = jnp.concatenate([taps[:1], taps[:0:-1]], axis=0).T
    scaled = residue * jnp.sqrt(-jnp.expm1(-2.0 * pole_rate))
    rate_t = pole_rate.T
    long_taps = jnp.sum(
        scaled.T[:, :, None] * jnp.exp(-rate_t[:, :, None] * backward.astype(F32)[None, None, :]), axis=1
    )
    position = jnp.arange(rows, dtype=F32)
    flat_rate = rate_t.reshape(-1)
    ending = jnp.exp(-flat_rate[:, None] * (rows - 1.0 - position)[None, :]).astype(BF16)
    entering = (jnp.exp(-flat_rate[None, :] * (position + 1.0)[:, None]) * scaled.T.reshape(1, -1)).astype(BF16)
    own_groups = owned // per_group
    own_rate = lax.dynamic_slice_in_dim(pole_rate, lax.axis_index("inner") * own_groups, own_groups, 1)
    own_rate = jnp.repeat(own_rate, per_group, axis=1)
    decay = jnp.exp(-own_rate * rows)
    team_decay = jnp.exp(-own_rate * (rows * members))

    full = shape((rows, width), BF16)
    block = pltpu.VMEM((rows, width), BF16)
    table = shape((width // LANES, LANES // per_group * SUB, LANES + SUB), BF16)
    table_block = pltpu.VMEM(table.shape, BF16)
    medium_table, long_table = call(
        functools.partial(table_kernel, per_group),
        (table, table),
        [VMEM, VMEM],
        (HBM, HBM),
        "tables",
        (table_block, table_block, sems((2,))),
        0,
        16 * rows * width,
    )(taps, long_taps)

    mixed_mr, gated, states = call(
        functools.partial(medium_kernel, per_group),
        (full, full, shape((members, poles, owned), BF16)),
        [HBM] * 9,
        (HBM, HBM, VMEM),
        "medium",
        (table_block,)
        + (block,) * 5
        + (pltpu.VMEM((width, rows), BF16),)
        + (block,) * 2
        + (pltpu.VMEM((rows, LANES), F32), sems((PARTS, 5)), sems((2,)), sems((2, PARTS))),
        16 * rows * rows * width,
        14 * rows * width,
    )(medium_table, rim, product, query_mr, resid, key_li, ending, long_table, entering)

    states = lax.all_to_all(states, "inner", 0, 0, tiled=True)
    total = call(total_kernel, shape((teams, poles, owned), BF16), [VMEM, VMEM], VMEM, "total", limit=SMALL)(
        states, decay
    )
    totals = lax.all_to_all(total, "outer", 0, 0, tiled=True)
    local, token = call(
        functools.partial(local_kernel, per_group),
        (shape((rows, width), F32), shape((8, LANES), F32)),
        [HBM, HBM, HBM],
        (HBM, VMEM),
        "local",
        (table_block, block, pltpu.VMEM((rows, width), F32), sems((PARTS, 2)), sems((PARTS,))),
        16 * rows * rows * width,
        14 * rows * width,
    )(long_table, gated, total)
    entered = call(
        enter_kernel,
        shape((members, poles, owned), BF16),
        [SMEM] + [VMEM] * 5,
        VMEM,
        "enter",
        limit=SMALL,
    )(lax.axis_index("outer").astype(jnp.int32).reshape(1), states, totals, decay, team_decay, token)
    entered = lax.all_to_all(entered, "inner", 0, 0, tiled=True)

    long_out = call(
        functools.partial(final_kernel, per_group),
        full,
        [HBM, VMEM, HBM, HBM],
        HBM,
        "final",
        (block, pltpu.VMEM((rows, width), F32), block, block, sems((PARTS, 3)), sems((PARTS,))),
    )(entering, entered, local, query_li)
    return (mixed_mr, long_out)


def solution(mesh):
    rows = P(AXES, None)
    return jax.shard_map(
        shards,
        mesh=mesh,
        in_specs=(rows,) * 6 + (P(), P(), P()),
        out_specs=(rows, rows),
        check_vma=False,
    )
```

profile of v0, /device:TPU:1, one launch (start us, length us, event | category | flops | bytes accessed | tf_op | source)
XLA Modules:
  0.0 78.7 jit_solution(12350609583468778102)
XLA Ops:
  0.6 0.0 copy-start.3
  0.6 0.0 copy-start.4
  0.7 0.0 copy-start.5
  0.7 1.8 %multiply_convert_fusion.1.product_hbm = bf16[128,4096]{1,0:T(8,128)(2,1)S(1)} fusion(bf16[128,4096]{1,0:T(8,128)(2,1)} %param.12, bf16[128,4096]{1,0:T(8,128)(2,1)} %param.11), kind=kLoop, calls=%fused_computation.2 | loop fusion | flops 2097152 | bytes 3145728 | tf_op jit(solution)/shard_map/convert_element_type | solution.py:322
  2.5 0.0 copy-start.1
  2.5 4.6 %collective-permute-start = (bf16[128,4096]{1,0:T(8,128)(2,1)S(1)}, bf16[128,4096]{1,0:T(8,128)(2,1)S(1)}, u32[]{:S(2)}, u32[]{:S(2)}) collective-permute-start(bf16[128,4096]{1,0:T(8,128)(2,1)S(1)} %multiply_convert_fusion.1.product_hbm), channel_id=1, source_target_pairs={{0,1},{1,2},{2,3},{3,4},{4,5},{5,6},{6,7},{7,8},{8,9},{9,10},{10,1... | collective-permute-start | bytes 3145736 | tf_op jit(solution)/shard_map/ppermute | solution.py:28
  7.1 0.0 copy-done.3
  7.2 0.0 copy-done.4
  7.2 0.0 copy-done.5
  7.2 0.1 copy.20
  7.3 0.1 copy.21
  7.4 0.1 copy.24
  7.5 0.2 rev.3
  7.7 0.1 copy.25
  7.9 0.1 neg.35
  8.0 2.3 %multiply_reduce_fusion.long_taps_ref = f32[256,128]{1,0:T(8,128)} fusion(f32[128]{0:T(128)S(1)} %fusion, f32[256,16]{1,0:T(8,128)S(1)} %copy.21, f32[256,16]{1,0:T(8,128)S(1)} %copy.20), kind=kLoop, calls=%fused_computation.3 | loop fusion | flops 1540096 | bytes 164352 | tf_op jit(solution)/shard_map/reduce_sum | solution.py:330
  10.3 1.5 %exponential_convert_fusion.ending_hbm = bf16[4096,128]{1,0:T(8,128)(2,1)} fusion(f32[128]{0:T(128)S(1)} %iota_subtract_fusion, f32[4096]{0:T(1024)S(1)} %neg.35), kind=kLoop, calls=%fused_computation.1 | loop fusion | flops 1048576 | bytes 1065472 | tf_op jit(solution)/shard_map/convert_element_type | solution.py:335
  11.8 0.8 maximum_bitcast_fusion.medium_taps_ref
  12.6 0.1 mul.103
  12.7 5.4 %tables.1 = (bf16[32,256,160]{2,1,0:T(8,128)(2,1)}, bf16[32,256,160]{2,1,0:T(8,128)(2,1)}) custom-call(f32[256,128]{1,0:T(8,128)} %maximum_bitcast_fusion.medium_taps_ref, f32[256,128]{1,0:T(8,128)} %multiply_reduce_fusion.long_taps_ref), custom_call_target="tpu_custom_call" | custom-call | bytes 8388608 | tf_op jit(solution)/shard_map/tables/pallas_call | solution.py:347
  18.1 0.0 copy-done.1
  18.1 1.4 %multiply_convert_fusion.entering_hbm = bf16[128,4096]{1,0:T(8,128)(2,1)} fusion(f32[4096]{0:T(1024)S(1)} %mul.103, f32[128]{0:T(128)S(1)} %iota_add_fusion, f32[4096]{0:T(1024)S(1)} %neg.35), kind=kLoop, calls=%fused_computation | loop fusion | flops 1572864 | bytes 1081856 | tf_op jit(solution)/shard_map/convert_element_type | solution.py:336
  19.6 0.0 collective-permute-done.rim_hbm
  19.6 0.0 copy-start.2
  19.6 1.0 %copy-done.2 = bf16[128,4096]{1,0:T(8,128)(2,1)} copy-done((bf16[128,4096]{1,0:T(8,128)(2,1)}, bf16[128,4096]{1,0:T(8,128)(2,1)S(1)}, u32[]{:S(2)}) %copy-start.2) | copy-done | bytes 1048600
  20.6 7.3 %medium.1 = (bf16[128,4096]{1,0:T(8,128)(2,1)}, bf16[128,4096]{1,0:T(8,128)(2,1)}, bf16[32,16,128]{2,1,0:T(8,128)(2,1)}) custom-call(bf16[32,256,160]{2,1,0:T(8,128)(2,1)} %get-tuple-element.9.table_hbm, bf16[128,4096]{1,0:T(8,128)(2,1)} %copy-done.2, bf16[128,4096]{1,0:T(8,128)(2,1)} %copy-done.1, bf16[128,4096]{1,0:T(8,128)(2,1)} %query_hbm.2, ...), custom_call_target="tpu_custom_call" | custom-call | flops 1073741824 | bytes 7340032 | tf_op jit(solution)/shard_map/medium/pallas_call | solution.py:358
  27.8 7.6 %all-to-all-start = ((bf16[32,16,128]{2,1,0:T(8,128)(2,1)}), bf16[32,16,128]{2,1,0:T(8,128)(2,1)S(1)}, u32[]{:S(2)}, u32[]{:S(2)}) async-start(bf16[32,16,128]{2,1,0:T(8,128)(2,1)} %get-tuple-element.12), calls=%async_computation | async-start | bytes 262144 | tf_op jit(solution)/shard_map/all_to_all | solution.py:373
  35.5 0.1 multiply_exponential_fusion
  35.6 0.1 broadcast_in_dim.4
  35.6 0.1 exp.23.decay_ref
  35.7 0.1 broadcast_in_dim.5
  35.8 0.1 exp.25.group_decay_ref
  35.9 7.3 %all-to-all-done.states_ref = bf16[32,16,128]{2,1,0:T(8,128)(2,1)S(1)} async-done(((bf16[32,16,128]{2,1,0:T(8,128)(2,1)}), bf16[32,16,128]{2,1,0:T(8,128)(2,1)S(1)}, u32[]{:S(2)}, u32[]{:S(2)}) %all-to-all-start) | async-done | bytes 131104 | tf_op jit(solution)/shard_map/all_to_all | solution.py:373
  43.2 0.7 total.1.after_ref
  43.9 10.1 %all-to-all-start.1 = ((bf16[8,16,128]{2,1,0:T(8,128)(2,1)}), bf16[8,16,128]{2,1,0:T(8,128)(2,1)S(1)}, u32[]{:S(2)}, u32[]{:S(2)}) async-start(bf16[8,16,128]{2,1,0:T(8,128)(2,1)} %total.1.after_ref), calls=%async_computation.1 | async-start | bytes 65536 | tf_op jit(solution)/shard_map/all_to_all | solution.py:377
  54.0 5.0 %local.1 = (f32[128,4096]{1,0:T(8,128)}, f32[8,128]{1,0:T(8,128)}) custom-call(bf16[32,256,160]{2,1,0:T(8,128)(2,1)} %get-tuple-element.10.long_hbm.table_hbm, bf16[128,4096]{1,0:T(8,128)(2,1)} %get-tuple-element.13.gated_hbm, bf16[8,16,128]{2,1,0:T(8,128)(2,1)} %total.1.after_ref), custom_call_target="tpu_custom_call" | custom-call | flops 1073741824 | bytes 7340032 | tf_op jit(solution)/shard_map/local/pallas_call | solution.py:378
  59.1 1.9 %all-to-all-done.1.totals_ref = bf16[8,16,128]{2,1,0:T(8,128)(2,1)S(1)} async-done(((bf16[8,16,128]{2,1,0:T(8,128)(2,1)}), bf16[8,16,128]{2,1,0:T(8,128)(2,1)S(1)}, u32[]{:S(2)}, u32[]{:S(2)}) %all-to-all-start.1) | async-done | bytes 32800 | tf_op jit(solution)/shard_map/all_to_all | solution.py:377
  61.0 0.0 copy-start
  61.0 0.7 copy-done
  61.6 0.1 enter.1
  61.7 12.8 %all_to_all.15.state_ref = bf16[32,16,128]{2,1,0:T(8,128)(2,1)} all-to-all(bf16[32,16,128]{2,1,0:T(8,128)(2,1)S(1)} %enter.1), channel_id=1, replica_groups=mesh['outer'=8,'inner'=32] {'inner'}, dimensions={0} | all-to-all | bytes 262144 | tf_op jit(solution)/shard_map/all_to_all | solution.py:396
  74.6 4.1 %final.1 = bf16[128,4096]{1,0:T(8,128)(2,1)} custom-call(bf16[128,4096]{1,0:T(8,128)(2,1)} %multiply_convert_fusion.entering_hbm, bf16[32,16,128]{2,1,0:T(8,128)(2,1)} %all_to_all.15.state_ref, f32[128,4096]{1,0:T(8,128)} %get-tuple-element.15.local_hbm, bf16[128,4096]{1,0:T(8,128)(2,1)} %query_hbm.3), custom_call_target="tpu_custom_call" | custom-call | tf_op jit(solution)/shard_map/final/pallas_call | solution.py:398
  (6 shorter events, 0.1 us)
Async XLA Ops:
  0.6 6.5 %copy-start.3 = (bf16[128,256]{1,0:T(8,128)(2,1)S(1)}, bf16[128,256]{1,0:T(8,128)(2,1)}, u32[]{:S(2)}) copy-start(bf16[128,256]{1,0:T(8,128)(2,1)} %param.15) | copy-start | bytes 196612
  0.6 6.5 %copy-start.4 = (f32[16,256]{1,0:T(8,128)S(1)}, f32[16,256]{1,0:T(8,128)}, u32[]{:S(2)}) copy-start(f32[16,256]{1,0:T(8,128)} %param.16) | copy-start | bytes 49156
  0.7 6.5 %copy-start.5 = (f32[16,256]{1,0:T(8,128)S(1)}, f32[16,256]{1,0:T(8,128)}, u32[]{:S(2)}) copy-start(f32[16,256]{1,0:T(8,128)} %param.17) | copy-start | bytes 49156
  2.5 15.6 %copy-start.1 = (bf16[128,4096]{1,0:T(8,128)(2,1)}, bf16[128,4096]{1,0:T(8,128)(2,1)S(1)}, u32[]{:S(2)}) copy-start(bf16[128,4096]{1,0:T(8,128)(2,1)S(1)} %multiply_convert_fusion.1.product_hbm) | copy-start | bytes 3145732
  2.5 17.1 %collective-permute-start = (bf16[128,4096]{1,0:T(8,128)(2,1)S(1)}, bf16[128,4096]{1,0:T(8,128)(2,1)S(1)}, u32[]{:S(2)}, u32[]{:S(2)}) collective-permute-start(bf16[128,4096]{1,0:T(8,128)(2,1)S(1)} %multiply_convert_fusion.1.product_hbm), channel_id=1, source_target_pairs={{0,1},{1,2},{2,3},{3,4},{4,5},{5,6},{6,7},{7,8},{8,9},{9,10},{10,1... | collective-permute-start | bytes 3145736 | tf_op jit(solution)/shard_map/ppermute | solution.py:28
  19.6 1.0 %copy-start.2 = (bf16[128,4096]{1,0:T(8,128)(2,1)}, bf16[128,4096]{1,0:T(8,128)(2,1)S(1)}, u32[]{:S(2)}) copy-start(bf16[128,4096]{1,0:T(8,128)(2,1)S(1)} %collective-permute-done.rim_hbm) | copy-start | bytes 3145732
  27.8 15.3 %all-to-all-start = ((bf16[32,16,128]{2,1,0:T(8,128)(2,1)}), bf16[32,16,128]{2,1,0:T(8,128)(2,1)S(1)}, u32[]{:S(2)}, u32[]{:S(2)}) async-start(bf16[32,16,128]{2,1,0:T(8,128)(2,1)} %get-tuple-element.12), calls=%async_computation | async-start | bytes 262144 | tf_op jit(solution)/shard_map/all_to_all | solution.py:373
  43.9 17.1 %all-to-all-start.1 = ((bf16[8,16,128]{2,1,0:T(8,128)(2,1)}), bf16[8,16,128]{2,1,0:T(8,128)(2,1)S(1)}, u32[]{:S(2)}, u32[]{:S(2)}) async-start(bf16[8,16,128]{2,1,0:T(8,128)(2,1)} %total.1.after_ref), calls=%async_computation.1 | async-start | bytes 65536 | tf_op jit(solution)/shard_map/all_to_all | solution.py:377
  61.0 0.7 copy-start
where the time goes:
time: 79.1 us; the launch traced here: 78.7 us
  Pallas kernels  22.6 us (29%)
  starting transfers between devices  22.4 us (28%)
  blocking collectives  12.8 us (16%)
  waiting for transfers between devices  9.19 us (12%)
  other arithmetic  8 us (10%)
  local copies, waits for them, and re-layouts  2.84 us (4%)
  between operations  0.83 us (1%)
    all_to_all x1, blocking collectives, shards(): entered = lax.all_to_all(entered, 'inner', 0, 0, tiled=True)  12.8 us
    all_to_all x1, starting transfers between devices, shards(): totals = lax.all_to_all(total, 'outer', 0, 0, tiled=True)  10.1 us
    all_to_all x1, starting transfers between devices, shards(): states = lax.all_to_all(states, 'inner', 0, 0, tiled=True)  7.62 us
    all_to_all x1, waiting for transfers between devices, shards(): states = lax.all_to_all(states, 'inner', 0, 0, tiled=True)  7.28 us
    pallas_call x1, Pallas kernels, shards(): call(functools.partial(medium_kernel, per_group), (full, full, shape((mem...  7.27 us
    pallas_call x1, Pallas kernels, shards(): call(functools.partial(table_kernel, per_group), (table, table), [VMEM, V...  5.44 us
    pallas_call x1, Pallas kernels, shards(): call(functools.partial(local_kernel, per_group), (shape((rows, width), F3...  5.05 us
    ppermute x1, starting transfers between devices, from_behind(): return lax.ppermute(block, axis, route)  4.59 us
  transfers between devices with their start and end apart: 3, of which 2 were waited for; matrix products, arithmetic and copies ran while one was open for 9% of the time, Pallas kernels for 13%

commit v1 on v0

--- a/solution.py
+++ b/solution.py
@@ -13,8 +13,7 @@
 HALF = LANES // 2
 SUB = 32
 PARTS = 4
-LARGE = 58 * 1024 * 1024
-SMALL = 4 * 1024 * 1024
+MIB = 1024 * 1024
 F32 = jnp.float32
 BF16 = jnp.bfloat16
 VMEM = pl.BlockSpec(memory_space=pltpu.VMEM)
@@ -295,7 +294,7 @@
         store(part).wait()
 
 
-def call(body, out, in_specs, out_specs, name, scratch=(), flops=0, moved=0, limit=LARGE):
+def call(body, out, in_specs, out_specs, name, scratch=(), flops=0, moved=0, limit=50 * MIB):
     return pl.pallas_call(
         body,
         out_shape=out,
@@ -353,6 +352,7 @@
         (table_block, table_block, sems((2,))),
         0,
         16 * rows * width,
+        12 * MIB,
     )(taps, long_taps)
 
     mixed_mr, gated, states = call(
@@ -371,7 +371,7 @@
     )(medium_table, rim, product, query_mr, resid, key_li, ending, long_table, entering)
 
     states = lax.all_to_all(states, "inner", 0, 0, tiled=True)
-    total = call(total_kernel, shape((teams, poles, owned), BF16), [VMEM, VMEM], VMEM, "total", limit=SMALL)(
+    total = call(total_kernel, shape((teams, poles, owned), BF16), [VMEM, VMEM], VMEM, "total", limit=4 * MIB)(
         states, decay
     )
     totals = lax.all_to_all(total, "outer", 0, 0, tiled=True)
@@ -391,7 +391,7 @@
         [SMEM] + [VMEM] * 5,
         VMEM,
         "enter",
-        limit=SMALL,
+        limit=4 * MIB,
     )(lax.axis_index("outer").astype(jnp.int32).reshape(1), states, totals, decay, team_decay, token)
     entered = lax.all_to_all(entered, "inner", 0, 0, tiled=True)
 

time: 79.1 us -> 74.8 us (0.946)
  Pallas kernels: 22.6 us -> 16.9 us
  local copies, waits for them, and re-layouts: 2.84 us -> 6.44 us
  other arithmetic: 8 us -> 6.68 us
    unnamed x14 -> x18, local copies, waits for them, and re-layouts: 1.9 us -> 5.5 us
    pallas_call x1, Pallas kernels: 5.44 us -> 3.1 us  [shards(): call(functools.partial(table_kernel, per_group), (table, table), [VMEM, V...]
    pallas_call x1, Pallas kernels: 4.14 us -> 2.93 us  [shards(): call(functools.partial(final_kernel, per_group), full, [HBM, VMEM, HBM, H...]
    pallas_call x1, Pallas kernels: 5.05 us -> 3.92 us  [shards(): call(functools.partial(local_kernel, per_group), (shape((rows, width), F3...]
    pallas_call x1, Pallas kernels: 7.27 us -> 6.16 us  [shards(): call(functools.partial(medium_kernel, per_group), (full, full, shape((mem...]
  transfers between devices with their start and end apart: 3 -> 3, of which waited for: 2 -> 2; matrix products, arithmetic and copies ran while one was open for 9% -> 8% of each run, Pallas kernels for 13% -> 9%
where the time goes in v1:
time: 74.8 us; the launch traced here: 74.5 us
  starting transfers between devices  22.1 us (30%)
  Pallas kernels  16.9 us (23%)
  blocking collectives  12.6 us (17%)
  waiting for transfers between devices  8.97 us (12%)
  other arithmetic  6.68 us (9%)
  local copies, waits for them, and re-layouts  6.44 us (9%)
  between operations  0.84 us (1%)
    all_to_all x1, blocking collectives, shards(): entered = lax.all_to_all(entered, 'inner', 0, 0, tiled=True)  12.6 us
    all_to_all x1, starting transfers between devices, shards(): totals = lax.all_to_all(total, 'outer', 0, 0, tiled=True)  10.1 us
    all_to_all x1, starting transfers between devices, shards(): states = lax.all_to_all(states, 'inner', 0, 0, tiled=True)  7.36 us
    all_to_all x1, waiting for transfers between devices, shards(): states = lax.all_to_all(states, 'inner', 0, 0, tiled=True)  7.28 us
    pallas_call x1, Pallas kernels, shards(): call(functools.partial(medium_kernel, per_group), (full, full, shape((mem...  6.16 us
    unnamed x18, local copies, waits for them, and re-layouts  5.5 us
    ppermute x1, starting transfers between devices, from_behind(): return lax.ppermute(block, axis, route)  4.59 us
    pallas_call x1, Pallas kernels, shards(): call(functools.partial(local_kernel, per_group), (shape((rows, width), F3...  3.92 us
  transfers between devices with their start and end apart: 3, of which 2 were waited for; matrix products, arithmetic and copies ran while one was open for 8% of the time, Pallas kernels for 9%

profile of v1, /device:TPU:1, one launch (start us, length us, event | category | flops | bytes accessed | tf_op | source)
XLA Modules:
  0.0 74.5 jit_solution(292231631958503675)
XLA Ops:
  0.6 0.0 copy-start.5
  0.6 0.0 copy-start.6
  0.7 0.0 copy-start.7
  0.7 1.8 %multiply_convert_fusion.1.product_hbm = bf16[128,4096]{1,0:T(8,128)(2,1)S(1)} fusion(bf16[128,4096]{1,0:T(8,128)(2,1)} %param.12, bf16[128,4096]{1,0:T(8,128)(2,1)} %param.11), kind=kLoop, calls=%fused_computation.2 | loop fusion | flops 2097152 | bytes 3145728 | tf_op jit(solution)/shard_map/convert_element_type | solution.py:321
  2.5 4.6 %collective-permute-start = (bf16[128,4096]{1,0:T(8,128)(2,1)S(1)}, bf16[128,4096]{1,0:T(8,128)(2,1)S(1)}, u32[]{:S(2)}, u32[]{:S(2)}) collective-permute-start(bf16[128,4096]{1,0:T(8,128)(2,1)S(1)} %multiply_convert_fusion.1.product_hbm), channel_id=1, source_target_pairs={{0,1},{1,2},{2,3},{3,4},{4,5},{5,6},{6,7},{7,8},{8,9},{9,10},{10,1... | collective-permute-start | bytes 3145736 | tf_op jit(solution)/shard_map/ppermute | solution.py:27
  7.1 0.0 copy-done.5
  7.2 0.0 copy-done.6
  7.2 0.0 copy-done.7
  7.2 0.1 copy.20
  7.3 0.1 copy.21
  7.4 0.1 copy.24
  7.5 0.2 rev.3
  7.7 0.1 copy.25
  7.9 0.1 neg.35
  8.0 1.7 %multiply_reduce_fusion.long_taps_ref = f32[256,128]{1,0:T(8,128)S(1)} fusion(f32[128]{0:T(128)S(1)} %fusion, f32[256,16]{1,0:T(8,128)S(1)} %copy.21, f32[256,16]{1,0:T(8,128)S(1)} %copy.20), kind=kLoop, calls=%fused_computation.3 | loop fusion | flops 1540096 | bytes 164352 | tf_op jit(solution)/shard_map/reduce_sum | solution.py:329
  9.6 1.5 %exponential_convert_fusion.ending_hbm = bf16[4096,128]{1,0:T(8,128)(2,1)} fusion(f32[128]{0:T(128)S(1)} %iota_subtract_fusion, f32[4096]{0:T(1024)S(1)} %neg.35), kind=kLoop, calls=%fused_computation.1 | loop fusion | flops 1048576 | bytes 1065472 | tf_op jit(solution)/shard_map/convert_element_type | solution.py:334
  11.2 0.1 maximum_bitcast_fusion.medium_taps_ref
  11.3 0.1 mul.103
  11.4 3.1 %tables.1 = (bf16[32,256,160]{2,1,0:T(8,128)(2,1)S(1)}, bf16[32,256,160]{2,1,0:T(8,128)(2,1)S(1)}) custom-call(f32[256,128]{1,0:T(8,128)S(1)} %maximum_bitcast_fusion.medium_taps_ref, f32[256,128]{1,0:T(8,128)S(1)} %multiply_reduce_fusion.long_taps_ref), custom_call_target="tpu_custom_call" | custom-call | bytes 8388608 | tf_op jit(solution)/shard_map/tables/pallas_call | solution.py:346
  14.5 0.0 copy-start
  14.5 1.9 %copy-done = bf16[32,256,160]{2,1,0:T(8,128)(2,1)} copy-done((bf16[32,256,160]{2,1,0:T(8,128)(2,1)}, bf16[32,256,160]{2,1,0:T(8,128)(2,1)S(1)}, u32[]{:S(2)}) %copy-start) | copy-done | bytes 2621464
  16.4 0.0 copy-start.2
  16.4 2.0 %copy-done.2 = bf16[32,256,160]{2,1,0:T(8,128)(2,1)} copy-done((bf16[32,256,160]{2,1,0:T(8,128)(2,1)}, bf16[32,256,160]{2,1,0:T(8,128)(2,1)S(1)}, u32[]{:S(2)}) %copy-start.2) | copy-done | bytes 2621464
  18.4 1.4 %multiply_convert_fusion.entering_hbm = bf16[128,4096]{1,0:T(8,128)(2,1)} fusion(f32[4096]{0:T(1024)S(1)} %mul.103, f32[128]{0:T(128)S(1)} %iota_add_fusion, f32[4096]{0:T(1024)S(1)} %neg.35), kind=kLoop, calls=%fused_computation | loop fusion | flops 1572864 | bytes 1081856 | tf_op jit(solution)/shard_map/convert_element_type | solution.py:335
  19.8 0.0 collective-permute-done.rim_hbm
  19.9 6.2 %medium.1 = (bf16[128,4096]{1,0:T(8,128)(2,1)}, bf16[128,4096]{1,0:T(8,128)(2,1)S(1)}, bf16[32,16,128]{2,1,0:T(8,128)(2,1)}) custom-call(bf16[32,256,160]{2,1,0:T(8,128)(2,1)} %copy-done.2, bf16[128,4096]{1,0:T(8,128)(2,1)S(1)} %collective-permute-done.rim_hbm, bf16[128,4096]{1,0:T(8,128)(2,1)S(1)} %multiply_convert_fusion.1.product_hbm, ...), custom_call_target="tpu_custom_call" | custom-call | flops 1073741824 | bytes 7340032 | tf_op jit(solution)/shard_map/medium/pallas_call | solution.py:358
  26.0 7.4 %all-to-all-start = ((bf16[32,16,128]{2,1,0:T(8,128)(2,1)}), bf16[32,16,128]{2,1,0:T(8,128)(2,1)S(1)}, u32[]{:S(2)}, u32[]{:S(2)}) async-start(bf16[32,16,128]{2,1,0:T(8,128)(2,1)} %get-tuple-element.12), calls=%async_computation | async-start | bytes 262144 | tf_op jit(solution)/shard_map/all_to_all | solution.py:373
  33.4 0.1 multiply_exponential_fusion
  33.5 0.1 broadcast_in_dim.4
  33.6 0.1 exp.23.decay_ref
  33.6 0.1 broadcast_in_dim.5
  33.7 0.1 exp.25.group_decay_ref
  33.8 7.3 %all-to-all-done.states_ref = bf16[32,16,128]{2,1,0:T(8,128)(2,1)S(1)} async-done(((bf16[32,16,128]{2,1,0:T(8,128)(2,1)}), bf16[32,16,128]{2,1,0:T(8,128)(2,1)S(1)}, u32[]{:S(2)}, u32[]{:S(2)}) %all-to-all-start) | async-done | bytes 131104 | tf_op jit(solution)/shard_map/all_to_all | solution.py:373
  41.1 0.7 total.1.after_ref
  41.8 10.1 %all-to-all-start.1 = ((bf16[8,16,128]{2,1,0:T(8,128)(2,1)}), bf16[8,16,128]{2,1,0:T(8,128)(2,1)S(1)}, u32[]{:S(2)}, u32[]{:S(2)}) async-start(bf16[8,16,128]{2,1,0:T(8,128)(2,1)} %total.1.after_ref), calls=%async_computation.1 | async-start | bytes 65536 | tf_op jit(solution)/shard_map/all_to_all | solution.py:377
  51.9 0.0 copy-start.1
  51.9 0.0 copy-start.4
  51.9 3.9 %local.1 = (f32[128,4096]{1,0:T(8,128)S(1)}, f32[8,128]{1,0:T(8,128)S(1)}) custom-call(bf16[32,256,160]{2,1,0:T(8,128)(2,1)} %copy-done, bf16[128,4096]{1,0:T(8,128)(2,1)S(1)} %get-tuple-element.13.gated_hbm, bf16[8,16,128]{2,1,0:T(8,128)(2,1)} %total.1.after_ref), custom_call_target="tpu_custom_call" | custom-call | flops 1073741824 | bytes 7340032 | tf_op jit(solution)/shard_map/local/pallas_call | solution.py:378
  55.9 0.0 copy-start.3
  55.9 1.3 %copy-done.3 = f32[128,4096]{1,0:T(8,128)} copy-done((f32[128,4096]{1,0:T(8,128)}, f32[128,4096]{1,0:T(8,128)S(1)}, u32[]{:S(2)}) %copy-start.3) | copy-done | bytes 2097176
  57.2 1.7 %all-to-all-done.1.totals_ref = bf16[8,16,128]{2,1,0:T(8,128)(2,1)S(1)} async-done(((bf16[8,16,128]{2,1,0:T(8,128)(2,1)}), bf16[8,16,128]{2,1,0:T(8,128)(2,1)S(1)}, u32[]{:S(2)}, u32[]{:S(2)}) %all-to-all-start.1) | async-done | bytes 32800 | tf_op jit(solution)/shard_map/all_to_all | solution.py:377
  58.9 0.1 enter.1
  59.0 12.6 %all_to_all.15.state_ref = bf16[32,16,128]{2,1,0:T(8,128)(2,1)S(1)} all-to-all(bf16[32,16,128]{2,1,0:T(8,128)(2,1)S(1)} %enter.1), channel_id=1, replica_groups=mesh['outer'=8,'inner'=32] {'inner'}, dimensions={0} | all-to-all | bytes 262144 | tf_op jit(solution)/shard_map/all_to_all | solution.py:396
  71.6 0.0 copy-done.1
  71.6 0.0 copy-done.4
  71.6 2.9 %final.1 = bf16[128,4096]{1,0:T(8,128)(2,1)} custom-call(bf16[128,4096]{1,0:T(8,128)(2,1)S(1)} %copy-done.1, bf16[32,16,128]{2,1,0:T(8,128)(2,1)S(1)} %all_to_all.15.state_ref, f32[128,4096]{1,0:T(8,128)} %copy-done.3, bf16[128,4096]{1,0:T(8,128)(2,1)S(1)} %copy-done.4), custom_call_target="tpu_custom_call" | custom-call | tf_op jit(solution)/shard_map/final/pallas_call | solution.py:398
  (6 shorter events, 0.1 us)
Async XLA Ops:
  0.6 6.5 %copy-start.5 = (bf16[128,256]{1,0:T(8,128)(2,1)S(1)}, bf16[128,256]{1,0:T(8,128)(2,1)}, u32[]{:S(2)}) copy-start(bf16[128,256]{1,0:T(8,128)(2,1)} %param.15) | copy-start | bytes 196612
  0.6 6.5 %copy-start.6 = (f32[16,256]{1,0:T(8,128)S(1)}, f32[16,256]{1,0:T(8,128)}, u32[]{:S(2)}) copy-start(f32[16,256]{1,0:T(8,128)} %param.16) | copy-start | bytes 49156
  0.7 6.5 %copy-start.7 = (f32[16,256]{1,0:T(8,128)S(1)}, f32[16,256]{1,0:T(8,128)}, u32[]{:S(2)}) copy-start(f32[16,256]{1,0:T(8,128)} %param.17) | copy-start | bytes 49156
  2.5 17.4 %collective-permute-start = (bf16[128,4096]{1,0:T(8,128)(2,1)S(1)}, bf16[128,4096]{1,0:T(8,128)(2,1)S(1)}, u32[]{:S(2)}, u32[]{:S(2)}) collective-permute-start(bf16[128,4096]{1,0:T(8,128)(2,1)S(1)} %multiply_convert_fusion.1.product_hbm), channel_id=1, source_target_pairs={{0,1},{1,2},{2,3},{3,4},{4,5},{5,6},{6,7},{7,8},{8,9},{9,10},{10,1... | collective-permute-start | bytes 3145736 | tf_op jit(solution)/shard_map/ppermute | solution.py:27
  14.5 2.0 %copy-start = (bf16[32,256,160]{2,1,0:T(8,128)(2,1)}, bf16[32,256,160]{2,1,0:T(8,128)(2,1)S(1)}, u32[]{:S(2)}) copy-start(bf16[32,256,160]{2,1,0:T(8,128)(2,1)S(1)} %get-tuple-element.10.long_hbm.table_hbm) | copy-start | bytes 7864324
  16.4 2.0 %copy-start.2 = (bf16[32,256,160]{2,1,0:T(8,128)(2,1)}, bf16[32,256,160]{2,1,0:T(8,128)(2,1)S(1)}, u32[]{:S(2)}) copy-start(bf16[32,256,160]{2,1,0:T(8,128)(2,1)S(1)} %get-tuple-element.9.table_hbm) | copy-start | bytes 7864324
  26.0 15.1 %all-to-all-start = ((bf16[32,16,128]{2,1,0:T(8,128)(2,1)}), bf16[32,16,128]{2,1,0:T(8,128)(2,1)S(1)}, u32[]{:S(2)}, u32[]{:S(2)}) async-start(bf16[32,16,128]{2,1,0:T(8,128)(2,1)} %get-tuple-element.12), calls=%async_computation | async-start | bytes 262144 | tf_op jit(solution)/shard_map/all_to_all | solution.py:373
  41.8 17.1 %all-to-all-start.1 = ((bf16[8,16,128]{2,1,0:T(8,128)(2,1)}), bf16[8,16,128]{2,1,0:T(8,128)(2,1)S(1)}, u32[]{:S(2)}, u32[]{:S(2)}) async-start(bf16[8,16,128]{2,1,0:T(8,128)(2,1)} %total.1.after_ref), calls=%async_computation.1 | async-start | bytes 65536 | tf_op jit(solution)/shard_map/all_to_all | solution.py:377
  51.9 19.6 %copy-start.1 = (bf16[128,4096]{1,0:T(8,128)(2,1)S(1)}, bf16[128,4096]{1,0:T(8,128)(2,1)}, u32[]{:S(2)}) copy-start(bf16[128,4096]{1,0:T(8,128)(2,1)} %multiply_convert_fusion.entering_hbm) | copy-start | bytes 3145732
  51.9 19.6 %copy-start.4 = (bf16[128,4096]{1,0:T(8,128)(2,1)S(1)}, bf16[128,4096]{1,0:T(8,128)(2,1)}, u32[]{:S(2)}) copy-start(bf16[128,4096]{1,0:T(8,128)(2,1)} %query_hbm.3) | copy-start | bytes 3145732
  55.9 1.3 %copy-start.3 = (f32[128,4096]{1,0:T(8,128)}, f32[128,4096]{1,0:T(8,128)S(1)}, u32[]{:S(2)}) copy-start(f32[128,4096]{1,0:T(8,128)S(1)} %get-tuple-element.15.local_hbm) | copy-start | bytes 6291460

commit v2 on v1

--- a/solution.py
+++ b/solution.py
@@ -97,8 +97,8 @@
         copy.wait()
 
 
-def medium_kernel(per_group, table_hbm, rim_hbm, product_hbm, query_hbm, resid_hbm, key_hbm, ending_hbm, long_hbm,
-                  entering_hbm, mixed_hbm, gated_hbm, state_ref, table_ref, rim_ref, product_ref, query_ref, resid_ref,
+def medium_kernel(per_group, table_hbm, rim_ref, product_ref, query_hbm, resid_hbm, key_hbm, ending_hbm, long_hbm,
+                  entering_hbm, mixed_hbm, gated_hbm, state_ref, table_ref, query_ref, resid_ref,
                   key_ref, ending_ref, mixed_ref, gated_ref, square_ref, load_sems, late_sems, store_sems):
     rows, width = product_ref.shape
     slabs = width // LANES // PARTS
@@ -109,9 +109,7 @@
         pairs = [(table_hbm.at[several], table_ref.at[several])]
         pairs += [
             (source.at[:, cols], target.at[:, cols])
-            for source, target in (
-                (rim_hbm, rim_ref), (product_hbm, product_ref), (query_hbm, query_ref), (resid_hbm, resid_ref)
-            )
+            for source, target in ((query_hbm, query_ref), (resid_hbm, resid_ref))
         ]
         return [pltpu.make_async_copy(*pair, load_sems.at[part, i]) for i, pair in enumerate(pairs)]
 
@@ -177,17 +175,15 @@
         store(gated_ref, gated_hbm, part, 1).wait()
 
 
-def local_kernel(per_group, table_hbm, gated_hbm, after_ref, local_hbm, token_ref, table_ref, gated_ref, local_ref,
+def local_kernel(per_group, table_hbm, gated_ref, after_ref, local_hbm, token_ref, table_ref, local_ref,
                  load_sems, store_sems):
     rows, width = gated_ref.shape
     slabs = width // LANES // PARTS
 
     def loads(part):
-        cols = span(part, width // PARTS)
         several = pl.ds(part * slabs, slabs)
         return [
             pltpu.make_async_copy(table_hbm.at[several], table_ref.at[several], load_sems.at[part, 0]),
-            pltpu.make_async_copy(gated_hbm.at[:, cols], gated_ref.at[:, cols], load_sems.at[part, 1]),
         ]
 
     def store(part):
@@ -245,8 +241,8 @@
             state = decay * state + states_ref[i].astype(F32)
 
 
-def final_kernel(per_group, entering_hbm, state_ref, local_hbm, query_hbm, out_hbm,
-                 entering_ref, local_ref, query_ref, out_ref, load_sems, store_sems):
+def final_kernel(per_group, entering_ref, state_ref, local_hbm, query_ref, out_hbm,
+                 local_ref, out_ref, load_sems, store_sems):
     owners, poles, owned = state_ref.shape
     width = owners * owned
     pair = 2
@@ -254,7 +250,7 @@
 
     def loads(part):
         cols = span(part, width // PARTS)
-        pairs = ((entering_hbm, entering_ref), (local_hbm, local_ref), (query_hbm, query_ref))
+        pairs = ((local_hbm, local_ref),)
         return [
             pltpu.make_async_copy(source.at[:, cols], target.at[:, cols], load_sems.at[part, i])
             for i, (source, target) in enumerate(pairs)
@@ -358,14 +354,14 @@
     mixed_mr, gated, states = call(
         functools.partial(medium_kernel, per_group),
         (full, full, shape((members, poles, owned), BF16)),
-        [HBM] * 9,
+        [HBM, VMEM, VMEM] + [HBM] * 6,
         (HBM, HBM, VMEM),
         "medium",
         (table_block,)
-        + (block,) * 5
+        + (block,) * 3
         + (pltpu.VMEM((width, rows), BF16),)
         + (block,) * 2
-        + (pltpu.VMEM((rows, LANES), F32), sems((PARTS, 5)), sems((2,)), sems((2, PARTS))),
+        + (pltpu.VMEM((rows, LANES), F32), sems((PARTS, 3)), sems((2,)), sems((2, PARTS))),
         16 * rows * rows * width,
         14 * rows * width,
     )(medium_table, rim, product, query_mr, resid, key_li, ending, long_table, entering)
@@ -378,10 +374,10 @@
     local, token = call(
         functools.partial(local_kernel, per_group),
         (shape((rows, width), F32), shape((8, LANES), F32)),
-        [HBM, HBM, HBM],
+        [HBM, VMEM, HBM],
         (HBM, VMEM),
         "local",
-        (table_block, block, pltpu.VMEM((rows, width), F32), sems((PARTS, 2)), sems((PARTS,))),
+        (table_block, pltpu.VMEM((rows, width), F32), sems((PARTS, 2)), sems((PARTS,))),
         16 * rows * rows * width,
         14 * rows * width,
     )(long_table, gated, total)
@@ -398,10 +394,10 @@
     long_out = call(
         functools.partial(final_kernel, per_group),
         full,
-        [HBM, VMEM, HBM, HBM],
+        [VMEM, VMEM, HBM, VMEM],
         HBM,
         "final",
-        (block, pltpu.VMEM((rows, width), F32), block, block, sems((PARTS, 3)), sems((PARTS,))),
+        (pltpu.VMEM((rows, width), F32), block, sems((PARTS, 1)), sems((PARTS,))),
     )(entering, entered, local, query_li)
     return (mixed_mr, long_out)
 

time: 74.8 us -> 74.6 us (level)
  no operation moved by 1% of the time
where the time goes in v2:
time: 74.6 us; the launch traced here: 74.3 us
  starting transfers between devices  22.1 us (30%)
  Pallas kernels  16.7 us (22%)
  blocking collectives  12.6 us (17%)
  waiting for transfers between devices  8.97 us (12%)
  other arithmetic  6.68 us (9%)
  local copies, waits for them, and re-layouts  6.44 us (9%)
  between operations  0.84 us (1%)
    all_to_all x1, blocking collectives, shards(): entered = lax.all_to_all(entered, 'inner', 0, 0, tiled=True)  12.6 us
    all_to_all x1, starting transfers between devices, shards(): totals = lax.all_to_all(total, 'outer', 0, 0, tiled=True)  10.1 us
    all_to_all x1, starting transfers between devices, shards(): states = lax.all_to_all(states, 'inner', 0, 0, tiled=True)  7.36 us
    all_to_all x1, waiting for transfers between devices, shards(): states = lax.all_to_all(states, 'inner', 0, 0, tiled=True)  7.28 us
    pallas_call x1, Pallas kernels, shards(): call(functools.partial(medium_kernel, per_group), (full, full, shape((mem...  6.07 us
    unnamed x18, local copies, waits for them, and re-layouts  5.5 us
    ppermute x1, starting transfers between devices, from_behind(): return lax.ppermute(block, axis, route)  4.59 us
    pallas_call x1, Pallas kernels, shards(): call(functools.partial(local_kernel, per_group), (shape((rows, width), F3...  3.92 us
  transfers between devices with their start and end apart: 3, of which 2 were waited for; matrix products, arithmetic and copies ran while one was open for 8% of the time, Pallas kernels for 9%

profile of v2, /device:TPU:1, one launch (start us, length us, event | category | flops | bytes accessed | tf_op | source)
XLA Modules:
  0.0 74.3 jit_solution(2204908738661789313)
XLA Ops:
  0.6 0.0 copy-start.5
  0.6 0.0 copy-start.6
  0.7 0.0 copy-start.7
  0.7 1.8 %multiply_convert_fusion.1.product_ref = bf16[128,4096]{1,0:T(8,128)(2,1)S(1)} fusion(bf16[128,4096]{1,0:T(8,128)(2,1)} %param.12, bf16[128,4096]{1,0:T(8,128)(2,1)} %param.11), kind=kLoop, calls=%fused_computation.2 | loop fusion | flops 2097152 | bytes 3145728 | tf_op jit(solution)/shard_map/convert_element_type | solution.py:317
  2.5 4.6 %collective-permute-start = (bf16[128,4096]{1,0:T(8,128)(2,1)S(1)}, bf16[128,4096]{1,0:T(8,128)(2,1)S(1)}, u32[]{:S(2)}, u32[]{:S(2)}) collective-permute-start(bf16[128,4096]{1,0:T(8,128)(2,1)S(1)} %multiply_convert_fusion.1.product_ref), channel_id=1, source_target_pairs={{0,1},{1,2},{2,3},{3,4},{4,5},{5,6},{6,7},{7,8},{8,9},{9,10},{10,1... | collective-permute-start | bytes 3145736 | tf_op jit(solution)/shard_map/ppermute | solution.py:27
  7.1 0.0 copy-done.5
  7.2 0.0 copy-done.6
  7.2 0.0 copy-done.7
  7.2 0.1 copy.20
  7.3 0.1 copy.21
  7.4 0.1 copy.24
  7.5 0.2 rev.3
  7.7 0.1 copy.25
  7.9 0.1 neg.35
  8.0 1.7 %multiply_reduce_fusion.long_taps_ref = f32[256,128]{1,0:T(8,128)S(1)} fusion(f32[128]{0:T(128)S(1)} %fusion, f32[256,16]{1,0:T(8,128)S(1)} %copy.21, f32[256,16]{1,0:T(8,128)S(1)} %copy.20), kind=kLoop, calls=%fused_computation.3 | loop fusion | flops 1540096 | bytes 164352 | tf_op jit(solution)/shard_map/reduce_sum | solution.py:325
  9.6 1.5 %exponential_convert_fusion.ending_hbm = bf16[4096,128]{1,0:T(8,128)(2,1)} fusion(f32[128]{0:T(128)S(1)} %iota_subtract_fusion, f32[4096]{0:T(1024)S(1)} %neg.35), kind=kLoop, calls=%fused_computation.1 | loop fusion | flops 1048576 | bytes 1065472 | tf_op jit(solution)/shard_map/convert_element_type | solution.py:330
  11.2 0.1 maximum_bitcast_fusion.medium_taps_ref
  11.3 0.1 mul.103
  11.4 3.1 %tables.1 = (bf16[32,256,160]{2,1,0:T(8,128)(2,1)S(1)}, bf16[32,256,160]{2,1,0:T(8,128)(2,1)S(1)}) custom-call(f32[256,128]{1,0:T(8,128)S(1)} %maximum_bitcast_fusion.medium_taps_ref, f32[256,128]{1,0:T(8,128)S(1)} %multiply_reduce_fusion.long_taps_ref), custom_call_target="tpu_custom_call" | custom-call | bytes 8388608 | tf_op jit(solution)/shard_map/tables/pallas_call | solution.py:342
  14.5 0.0 copy-start
  14.5 1.9 %copy-done = bf16[32,256,160]{2,1,0:T(8,128)(2,1)} copy-done((bf16[32,256,160]{2,1,0:T(8,128)(2,1)}, bf16[32,256,160]{2,1,0:T(8,128)(2,1)S(1)}, u32[]{:S(2)}) %copy-start) | copy-done | bytes 2621464
  16.4 0.0 copy-start.2
  16.4 2.0 %copy-done.2 = bf16[32,256,160]{2,1,0:T(8,128)(2,1)} copy-done((bf16[32,256,160]{2,1,0:T(8,128)(2,1)}, bf16[32,256,160]{2,1,0:T(8,128)(2,1)S(1)}, u32[]{:S(2)}) %copy-start.2) | copy-done | bytes 2621464
  18.4 1.4 %multiply_convert_fusion.entering_hbm.entering_ref = bf16[128,4096]{1,0:T(8,128)(2,1)} fusion(f32[4096]{0:T(1024)S(1)} %mul.103, f32[128]{0:T(128)S(1)} %iota_add_fusion, f32[4096]{0:T(1024)S(1)} %neg.35), kind=kLoop, calls=%fused_computation | loop fusion | flops 1572864 | bytes 1081856 | tf_op jit(solution)/shard_map/convert_element_type | solution.py:331
  19.8 0.0 collective-permute-done.rim_ref
  19.9 6.1 %medium.1 = (bf16[128,4096]{1,0:T(8,128)(2,1)}, bf16[128,4096]{1,0:T(8,128)(2,1)S(1)}, bf16[32,16,128]{2,1,0:T(8,128)(2,1)}) custom-call(bf16[32,256,160]{2,1,0:T(8,128)(2,1)} %copy-done.2, bf16[128,4096]{1,0:T(8,128)(2,1)S(1)} %collective-permute-done.rim_ref, bf16[128,4096]{1,0:T(8,128)(2,1)S(1)} %multiply_convert_fusion.1.product_ref, ...), custom_call_target="tpu_custom_call" | custom-call | flops 1073741824 | bytes 7340032 | tf_op jit(solution)/shard_map/medium/pallas_call | solution.py:354
  25.9 7.4 %all-to-all-start = ((bf16[32,16,128]{2,1,0:T(8,128)(2,1)}), bf16[32,16,128]{2,1,0:T(8,128)(2,1)S(1)}, u32[]{:S(2)}, u32[]{:S(2)}) async-start(bf16[32,16,128]{2,1,0:T(8,128)(2,1)} %get-tuple-element.12), calls=%async_computation | async-start | bytes 262144 | tf_op jit(solution)/shard_map/all_to_all | solution.py:369
  33.3 0.1 multiply_exponential_fusion
  33.4 0.1 broadcast_in_dim.4
  33.5 0.1 exp.23.decay_ref
  33.6 0.1 broadcast_in_dim.5
  33.6 0.1 exp.25.group_decay_ref
  33.7 7.3 %all-to-all-done.states_ref = bf16[32,16,128]{2,1,0:T(8,128)(2,1)S(1)} async-done(((bf16[32,16,128]{2,1,0:T(8,128)(2,1)}), bf16[32,16,128]{2,1,0:T(8,128)(2,1)S(1)}, u32[]{:S(2)}, u32[]{:S(2)}) %all-to-all-start) | async-done | bytes 131104 | tf_op jit(solution)/shard_map/all_to_all | solution.py:369
  41.0 0.7 total.1.after_ref
  41.7 10.1 %all-to-all-start.1 = ((bf16[8,16,128]{2,1,0:T(8,128)(2,1)}), bf16[8,16,128]{2,1,0:T(8,128)(2,1)S(1)}, u32[]{:S(2)}, u32[]{:S(2)}) async-start(bf16[8,16,128]{2,1,0:T(8,128)(2,1)} %total.1.after_ref), calls=%async_computation.1 | async-start | bytes 65536 | tf_op jit(solution)/shard_map/all_to_all | solution.py:373
  51.8 0.0 copy-start.1
  51.8 0.0 copy-start.4
  51.9 3.9 %local.1 = (f32[128,4096]{1,0:T(8,128)S(1)}, f32[8,128]{1,0:T(8,128)S(1)}) custom-call(bf16[32,256,160]{2,1,0:T(8,128)(2,1)} %copy-done, bf16[128,4096]{1,0:T(8,128)(2,1)S(1)} %get-tuple-element.13.gated_ref, bf16[8,16,128]{2,1,0:T(8,128)(2,1)} %total.1.after_ref), custom_call_target="tpu_custom_call" | custom-call | flops 1073741824 | bytes 7340032 | tf_op jit(solution)/shard_map/local/pallas_call | solution.py:374
  55.8 0.0 copy-start.3
  55.8 1.3 %copy-done.3 = f32[128,4096]{1,0:T(8,128)} copy-done((f32[128,4096]{1,0:T(8,128)}, f32[128,4096]{1,0:T(8,128)S(1)}, u32[]{:S(2)}) %copy-start.3) | copy-done | bytes 2097176
  57.1 1.7 %all-to-all-done.1.totals_ref = bf16[8,16,128]{2,1,0:T(8,128)(2,1)S(1)} async-done(((bf16[8,16,128]{2,1,0:T(8,128)(2,1)}), bf16[8,16,128]{2,1,0:T(8,128)(2,1)S(1)}, u32[]{:S(2)}, u32[]{:S(2)}) %all-to-all-start.1) | async-done | bytes 32800 | tf_op jit(solution)/shard_map/all_to_all | solution.py:373
  58.8 0.1 enter.1
  58.9 12.6 %all_to_all.15.state_ref = bf16[32,16,128]{2,1,0:T(8,128)(2,1)S(1)} all-to-all(bf16[32,16,128]{2,1,0:T(8,128)(2,1)S(1)} %enter.1), channel_id=1, replica_groups=mesh['outer'=8,'inner'=32] {'inner'}, dimensions={0} | all-to-all | bytes 262144 | tf_op jit(solution)/shard_map/all_to_all | solution.py:392
  71.5 0.0 copy-done.1
  71.5 0.0 copy-done.4
  71.5 2.8 %final.1 = bf16[128,4096]{1,0:T(8,128)(2,1)} custom-call(bf16[128,4096]{1,0:T(8,128)(2,1)S(1)} %copy-done.1, bf16[32,16,128]{2,1,0:T(8,128)(2,1)S(1)} %all_to_all.15.state_ref, f32[128,4096]{1,0:T(8,128)} %copy-done.3, bf16[128,4096]{1,0:T(8,128)(2,1)S(1)} %copy-done.4), custom_call_target="tpu_custom_call" | custom-call | tf_op jit(solution)/shard_map/final/pallas_call | solution.py:394
  (6 shorter events, 0.1 us)
Async XLA Ops:
  0.6 6.5 %copy-start.5 = (bf16[128,256]{1,0:T(8,128)(2,1)S(1)}, bf16[128,256]{1,0:T(8,128)(2,1)}, u32[]{:S(2)}) copy-start(bf16[128,256]{1,0:T(8,128)(2,1)} %param.15) | copy-start | bytes 196612
  0.6 6.5 %copy-start.6 = (f32[16,256]{1,0:T(8,128)S(1)}, f32[16,256]{1,0:T(8,128)}, u32[]{:S(2)}) copy-start(f32[16,256]{1,0:T(8,128)} %param.16) | copy-start | bytes 49156
  0.7 6.5 %copy-start.7 = (f32[16,256]{1,0:T(8,128)S(1)}, f32[16,256]{1,0:T(8,128)}, u32[]{:S(2)}) copy-start(f32[16,256]{1,0:T(8,128)} %param.17) | copy-start | bytes 49156
  2.5 17.4 %collective-permute-start = (bf16[128,4096]{1,0:T(8,128)(2,1)S(1)}, bf16[128,4096]{1,0:T(8,128)(2,1)S(1)}, u32[]{:S(2)}, u32[]{:S(2)}) collective-permute-start(bf16[128,4096]{1,0:T(8,128)(2,1)S(1)} %multiply_convert_fusion.1.product_ref), channel_id=1, source_target_pairs={{0,1},{1,2},{2,3},{3,4},{4,5},{5,6},{6,7},{7,8},{8,9},{9,10},{10,1... | collective-permute-start | bytes 3145736 | tf_op jit(solution)/shard_map/ppermute | solution.py:27
  14.5 2.0 %copy-start = (bf16[32,256,160]{2,1,0:T(8,128)(2,1)}, bf16[32,256,160]{2,1,0:T(8,128)(2,1)S(1)}, u32[]{:S(2)}) copy-start(bf16[32,256,160]{2,1,0:T(8,128)(2,1)S(1)} %get-tuple-element.10.long_hbm.table_hbm) | copy-start | bytes 7864324
  16.4 2.0 %copy-start.2 = (bf16[32,256,160]{2,1,0:T(8,128)(2,1)}, bf16[32,256,160]{2,1,0:T(8,128)(2,1)S(1)}, u32[]{:S(2)}) copy-start(bf16[32,256,160]{2,1,0:T(8,128)(2,1)S(1)} %get-tuple-element.9.table_hbm) | copy-start | bytes 7864324
  25.9 15.1 %all-to-all-start = ((bf16[32,16,128]{2,1,0:T(8,128)(2,1)}), bf16[32,16,128]{2,1,0:T(8,128)(2,1)S(1)}, u32[]{:S(2)}, u32[]{:S(2)}) async-start(bf16[32,16,128]{2,1,0:T(8,128)(2,1)} %get-tuple-element.12), calls=%async_computation | async-start | bytes 262144 | tf_op jit(solution)/shard_map/all_to_all | solution.py:369
  41.7 17.1 %all-to-all-start.1 = ((bf16[8,16,128]{2,1,0:T(8,128)(2,1)}), bf16[8,16,128]{2,1,0:T(8,128)(2,1)S(1)}, u32[]{:S(2)}, u32[]{:S(2)}) async-start(bf16[8,16,128]{2,1,0:T(8,128)(2,1)} %total.1.after_ref), calls=%async_computation.1 | async-start | bytes 65536 | tf_op jit(solution)/shard_map/all_to_all | solution.py:373
  51.8 19.6 %copy-start.1 = (bf16[128,4096]{1,0:T(8,128)(2,1)S(1)}, bf16[128,4096]{1,0:T(8,128)(2,1)}, u32[]{:S(2)}) copy-start(bf16[128,4096]{1,0:T(8,128)(2,1)} %multiply_convert_fusion.entering_hbm.entering_ref) | copy-start | bytes 3145732
  51.8 19.6 %copy-start.4 = (bf16[128,4096]{1,0:T(8,128)(2,1)S(1)}, bf16[128,4096]{1,0:T(8,128)(2,1)}, u32[]{:S(2)}) copy-start(bf16[128,4096]{1,0:T(8,128)(2,1)} %query_ref.1) | copy-start | bytes 3145732
  55.8 1.3 %copy-start.3 = (f32[128,4096]{1,0:T(8,128)}, f32[128,4096]{1,0:T(8,128)S(1)}, u32[]{:S(2)}) copy-start(f32[128,4096]{1,0:T(8,128)S(1)} %get-tuple-element.15.local_hbm) | copy-start | bytes 6291460
